TPU v7x, 32 devices: a whole 2x2x4 slice. The times are simulated.
32 devices in a mesh: grp: 2 (over y), exp: 16 (over z, x, core).
Axes of the slice: x: 2, y: 2, z: 4, core: 2. Of those that a mesh axis runs over, the one named last changes fastest.
Arguments:
- output_gradient: bfloat16 [512, 2048], P(('grp', 'exp')), parts along dimension 0, may hold values from -6 to 6
- input_tokens: bfloat16 [512, 2048], P(('grp', 'exp')), parts along dimension 0, may hold values from -6 to 6
- routes: int32 [512, 8], P(('grp', 'exp')), parts along dimension 0, may hold values from 0 to 15, all different within a row; in each aligned block of 16 rows (0 to 15, 16 to 31, ...) at most 16 rows name the same one
- combine: bfloat16 [512, 8], P(('grp', 'exp')), parts along dimension 0, may hold values from 0.019897461 to 0.5
- gate_matrix: bfloat16 [16, 2048, 768], P('exp'), may hold values from -0.125 to 0.125
- upward_matrix: bfloat16 [16, 2048, 768], P('exp'), may hold values from -0.125 to 0.125
- down_matrix: bfloat16 [16, 768, 2048], P('exp'), may hold values from -0.21875 to 0.21875
- gate_adapter_left: bfloat16 [2048, 16], replicated, may hold values from -0.125 to 0.125
- gate_adapter_right: bfloat16 [16, 768], replicated, may hold values from -0.375 to 0.375
- upward_adapter_left: bfloat16 [2048, 16], replicated, may hold values from -0.125 to 0.125
- upward_adapter_right: bfloat16 [16, 768], replicated, may hold values from -0.375 to 0.375
- down_adapter_left: bfloat16 [768, 16], replicated, may hold values from -0.21875 to 0.21875
- down_adapter_right: bfloat16 [16, 2048], replicated, may hold values from -0.375 to 0.375
Outputs:
- grad_in: bfloat16 [512, 2048], P(('grp', 'exp')), parts along dimension 0
- grad_combine: bfloat16 [512, 8], P(('grp', 'exp')), parts along dimension 0
- grad_adapters: float32 [270336], P(('grp', 'exp')), parts along dimension 0
There are 2 independent parts, one for each index of `grp`. A program takes and returns all parts, laid end to end along the dimension named above; an argument that names none is the same for every part. Nothing has to cross between parts.
Inputs may be any that keep to these rules, and one draw needn't show every extreme that they name: `routes`: within each aligned block of 16 rows (the tokens of one device) no expert is named more than 16 times; in every draw some block names some expert exactly 16 times. A row names 8 different experts.
All inputs are finite; a program needn't handle non-finite values.
Results may differ from a plain program's by a relative error of at most 0.0085.
Values may be sent and summed in bfloat16 or wider, within the bound.
A program may use at most 64 MiB of HBM per device.

v0:
```python
import jax
import jax.numpy as jnp
from jax import lax
from jax.sharding import PartitionSpec as P

adapter_scale = 2.0


def expert_forward_pass(
    incoming_rows,
    gate_matrix,
    upward_matrix,
    gate_adapter_left,
    gate_adapter_right,
    upward_adapter_left,
    upward_adapter_right,
    down_adapter_left,
):
    lowrank_gate = jnp.dot(
        incoming_rows, gate_adapter_left, preferred_element_type=jnp.float32
    ).astype(jnp.bfloat16)
    lowrank_upward = jnp.dot(
        incoming_rows, upward_adapter_left, preferred_element_type=jnp.float32
    ).astype(jnp.bfloat16)
    gate_preactivation = jnp.dot(
        incoming_rows, gate_matrix, preferred_element_type=jnp.float32
    ) + adapter_scale * jnp.dot(
        lowrank_gate, gate_adapter_right, preferred_element_type=jnp.float32
    )
    upward_preactivation = jnp.dot(
        incoming_rows, upward_matrix, preferred_element_type=jnp.float32
    ) + adapter_scale * jnp.dot(
        lowrank_upward, upward_adapter_right, preferred_element_type=jnp.float32
    )
    hidden_activation = (jax.nn.silu(gate_preactivation) * upward_preactivation).astype(
        jnp.bfloat16
    )
    lowrank_hidden = jnp.dot(
        hidden_activation, down_adapter_left, preferred_element_type=jnp.float32
    ).astype(jnp.bfloat16)
    return (
        lowrank_gate,
        lowrank_upward,
        gate_preactivation,
        upward_preactivation,
        hidden_activation,
        lowrank_hidden,
    )


def expert_reverse_pass(
    saved_activations,
    incoming_rows,
    gradient_rows,
    gate_row_values,
    gate_matrix,
    upward_matrix,
    down_matrix,
    gate_adapter_left,
    gate_adapter_right,
    upward_adapter_left,
    upward_adapter_right,
    down_adapter_left,
    down_adapter_right,
):
    (
        lowrank_gate,
        lowrank_upward,
        gate_preactivation,
        upward_preactivation,
        hidden_activation,
        lowrank_hidden,
    ) = saved_activations
    backward_lowrank = jnp.dot(
        gradient_rows, down_adapter_right.T, preferred_element_type=jnp.float32
    )
    backward_truncated = backward_lowrank.astype(jnp.bfloat16)
    hidden_unscaled = jnp.dot(
        gradient_rows, down_matrix.T, preferred_element_type=jnp.float32
    ) + adapter_scale * jnp.dot(
        backward_truncated, down_adapter_left.T, preferred_element_type=jnp.float32
    )
    weight_row_values = jnp.sum(
        hidden_activation.astype(jnp.float32) * hidden_unscaled, axis=1
    ).astype(jnp.bfloat16)
    scales = gate_row_values.astype(jnp.float32)[:, None]
    hidden_grad = scales * hidden_unscaled
    logistic = jax.nn.sigmoid(gate_preactivation)
    gate_gradient = (
        hidden_grad
        * upward_preactivation
        * logistic
        * (1.0 + gate_preactivation * (1.0 - logistic))
    ).astype(jnp.bfloat16)
    upward_gradient = (hidden_grad * gate_preactivation * logistic).astype(jnp.bfloat16)
    gate_reverse = jnp.dot(
        gate_gradient, gate_adapter_right.T, preferred_element_type=jnp.float32
    ).astype(jnp.bfloat16)
    upward_reverse = jnp.dot(
        upward_gradient, upward_adapter_right.T, preferred_element_type=jnp.float32
    ).astype(jnp.bfloat16)
    input_row_values = jnp.dot(
        gate_gradient, gate_matrix.T, preferred_element_type=jnp.float32
    ) + jnp.dot(upward_gradient, upward_matrix.T, preferred_element_type=jnp.float32)
    input_row_values = input_row_values + adapter_scale * (
        jnp.dot(gate_reverse, gate_adapter_left.T, preferred_element_type=jnp.float32)
        + jnp.dot(upward_reverse, upward_adapter_left.T, preferred_element_type=jnp.float32)
    )
    input_row_values = input_row_values.astype(jnp.bfloat16)
    scaled_rows = (scales * gradient_rows.astype(jnp.float32)).astype(jnp.bfloat16)
    scaled_low = (scales * backward_lowrank).astype(jnp.bfloat16)
    partial_results = [
        jnp.dot(incoming_rows.T, gate_reverse, preferred_element_type=jnp.float32),
        jnp.dot(lowrank_gate.T, gate_gradient, preferred_element_type=jnp.float32),
        jnp.dot(incoming_rows.T, upward_reverse, preferred_element_type=jnp.float32),
        jnp.dot(lowrank_upward.T, upward_gradient, preferred_element_type=jnp.float32),
        jnp.dot(hidden_activation.T, scaled_low, preferred_element_type=jnp.float32),
        jnp.dot(lowrank_hidden.T, scaled_rows, preferred_element_type=jnp.float32),
    ]
    adapter_products = adapter_scale * jnp.concatenate(
        [partial_result.reshape(-1) for partial_result in partial_results]
    )
    return (input_row_values, weight_row_values, adapter_products)


def shards(
    output_gradient,
    input_tokens,
    routes,
    combine,
    gate_matrix,
    upward_matrix,
    down_matrix,
    gate_adapter_left,
    gate_adapter_right,
    upward_adapter_left,
    upward_adapter_right,
    down_adapter_left,
    down_adapter_right,
):
    devices = lax.axis_size("exp")
    token_rows, model_width = output_gradient.shape
    top_k = routes.shape[1]
    capacity = max(2, min(token_rows, (2 * token_rows * top_k + devices - 1) // devices))
    slots_total = devices * capacity
    chosen = routes.reshape(-1)
    onehot = (chosen[:, None] == jnp.arange(devices, dtype=jnp.int32)[None, :]).astype(jnp.int32)
    earlier = jnp.cumsum(onehot, axis=0) - onehot
    target = chosen * capacity + jnp.sum(earlier * onehot, axis=1)
    owners = jnp.arange(chosen.shape[0], dtype=jnp.int32) // top_k
    send_inputs = (
        jnp.zeros((slots_total, model_width), jnp.bfloat16)
        .at[target]
        .set(input_tokens[owners])
        .reshape(devices, capacity, model_width)
    )
    send_grads = (
        jnp.zeros((slots_total, model_width), jnp.bfloat16)
        .at[target]
        .set(output_gradient[owners])
        .reshape(devices, capacity, model_width)
    )
    send_gates = (
        jnp.zeros((slots_total,), jnp.bfloat16)
        .at[target]
        .set(combine.reshape(-1))
        .reshape(devices, capacity)
    )
    gate_local = gate_matrix[0]
    upper_local = upward_matrix[0]
    down_local = down_matrix[0]
    got_inputs = lax.all_to_all(
        send_inputs, "exp", split_axis=0, concat_axis=0, tiled=True
    ).reshape(slots_total, model_width)
    saved_activations = expert_forward_pass(
        got_inputs,
        gate_local,
        upper_local,
        gate_adapter_left,
        gate_adapter_right,
        upward_adapter_left,
        upward_adapter_right,
        down_adapter_left,
    )
    got_grads, got_gates = (
        lax.all_to_all(send_grads, "exp", split_axis=0, concat_axis=0, tiled=True),
        lax.all_to_all(send_gates, "exp", split_axis=0, concat_axis=0, tiled=True),
    )
    got_grads = got_grads.reshape(slots_total, model_width)
    got_gates = got_gates.reshape(slots_total)
    input_row_values, weight_row_values, adapter_products = expert_reverse_pass(
        saved_activations,
        got_inputs,
        got_grads,
        got_gates,
        gate_local,
        upper_local,
        down_local,
        gate_adapter_left,
        gate_adapter_right,
        upward_adapter_left,
        upward_adapter_right,
        down_adapter_left,
        down_adapter_right,
    )
    back_inputs, back_weights = (
        lax.all_to_all(
            input_row_values.reshape(devices, capacity, model_width),
            "exp",
            split_axis=0,
            concat_axis=0,
            tiled=True,
        ),
        lax.all_to_all(
            weight_row_values.reshape(devices, capacity),
            "exp",
            split_axis=0,
            concat_axis=0,
            tiled=True,
        ),
    )
    returned = back_inputs.reshape(slots_total, model_width)[target].reshape(
        token_rows, top_k, model_width
    )
    grad_in = jnp.sum(returned.astype(jnp.float32), axis=1).astype(jnp.bfloat16)
    grad_combine = back_weights.reshape(slots_total)[target].reshape(token_rows, top_k)
    summed = lax.psum(adapter_products, "exp")
    share_length = adapter_products.shape[0] // devices
    grad_adapters = lax.dynamic_slice_in_dim(
        summed, lax.axis_index("exp") * share_length, share_length
    )
    return (grad_in, grad_combine, grad_adapters)


def solution(mesh):
    placed = (
        P(("grp", "exp"), None),
        P(("grp", "exp"), None),
        P(("grp", "exp"), None),
        P(("grp", "exp"), None),
        P("exp", None, None),
        P("exp", None, None),
        P("exp", None, None),
        P(),
        P(),
        P(),
        P(),
        P(),
        P(),
    )
    return jax.shard_map(
        shards,
        mesh=mesh,
        in_specs=placed,
        out_specs=(P(("grp", "exp"), None), P(("grp", "exp"), None), P(("grp", "exp"))),
        check_vma=False,
    )
```

profile of v0, /device:TPU:0, one launch (start us, length us, event | category | flops | bytes accessed | tf_op | source)
XLA Modules:
  0.0 264.4 jit_solution(837337535507671372)
XLA Ops:
  7.2 0.9 copy.28
  8.1 0.7 broadcast_multiply_fusion.1
  8.9 0.1 fusion.26
  9.0 0.2 reduce_window_sum.11
  9.2 0.2 select_reduce_fusion
  9.4 0.1 mul.93
  9.5 0.8 copy.29
  10.3 0.1 reshape.209
  10.4 1.3 scatter_custom_fusion
  11.8 0.7 all_to_all.25
  12.4 7.4 %all-to-all-start = ((bf16[16,1,16]{2,1,0:T(2,128)(2,1)}), bf16[16,1,16]{2,1,0:T(2,128)(2,1)S(1)}, u32[]{:S(2)}, u32[]{:S(2)}) async-start(bf16[16,1,16]{2,1,0:T(2,128)(2,1)} %all_to_all.25), calls=%async_computation | async-start | bytes 16384 | tf_op jit(solution)/shard_map/all_to_all | solution.py:187
  19.9 5.1 %scatter_custom_fusion.2 = bf16[256,2048]{1,0:T(8,128)(2,1)} fusion(s32[128]{0:T(128)S(1)} %fusion.31, bf16[16,2048]{1,0:T(8,128)(2,1)} %param.14, s32[1024]{0:T(1024)S(1)} %pad_clamp_fusion.1, bf16[]{:T(256)} %constant.16.clone.1), kind=kCustom, calls=%fused_computation.42 | custom fusion | bytes 1049088 | tf_op jit(solution)/shard_map/scatter | solution.py:154
  24.9 1.2 all-to-all-done
  26.1 5.0 %all-to-all-start.2 = ((bf16[16,16,2048]{2,1,0:T(8,128)(2,1)}), bf16[16,16,2048]{2,1,0:T(8,128)(2,1)}, u32[]{:S(2)}, u32[]{:S(2)}) async-start(bf16[16,16,2048]{2,1,0:T(8,128)(2,1)} %bitcast.70), calls=%async_computation.2 | async-start | bytes 2097152 | tf_op jit(solution)/shard_map/all_to_all | solution.py:172
  31.1 5.2 %scatter_custom_fusion.1 = bf16[256,2048]{1,0:T(8,128)(2,1)} fusion(s32[128]{0:T(128)S(1)} %fusion.31, bf16[16,2048]{1,0:T(8,128)(2,1)} %param.13, s32[1024]{0:T(1024)S(1)} %pad_clamp_fusion.1, bf16[]{:T(256)} %constant.16.clone.1), kind=kCustom, calls=%fused_computation.44 | custom fusion | bytes 1049088 | tf_op jit(solution)/shard_map/scatter | solution.py:160
  36.3 17.8 %all-to-all-done.2 = bf16[16,16,2048]{2,1,0:T(8,128)(2,1)} async-done(((bf16[16,16,2048]{2,1,0:T(8,128)(2,1)}), bf16[16,16,2048]{2,1,0:T(8,128)(2,1)}, u32[]{:S(2)}, u32[]{:S(2)}) %all-to-all-start.2) | async-done | bytes 1048608 | tf_op jit(solution)/shard_map/all_to_all | solution.py:172
  54.1 6.9 %all-to-all-start.1 = ((bf16[16,16,2048]{2,1,0:T(8,128)(2,1)}), bf16[16,16,2048]{2,1,0:T(8,128)(2,1)}, u32[]{:S(2)}, u32[]{:S(2)}) async-start(bf16[16,16,2048]{2,1,0:T(8,128)(2,1)} %bitcast.69), calls=%async_computation.1 | async-start | bytes 2097152 | tf_op jit(solution)/shard_map/all_to_all | solution.py:186
  61.1 0.6 reshape.172
  61.8 1.6 convolution_convert_fusion
  63.4 1.7 convolution_convert_fusion.1
  65.1 3.1 %fusion.2 = f32[256,768]{1,0:T(8,128)} fusion(bf16[256,2048]{1,0:T(8,128)(2,1)} %bitcast.7, bf16[1,2048,768]{2,1,0:T(8,128)(2,1)S(1)} %copy-done), kind=kOutput, calls=%fused_computation.9 | convolution fusion | flops 805306368 | bytes 4980736 | tf_op jit(solution)/shard_map/dot_general | solution.py:25
  68.2 3.1 %fusion.6 = f32[256,768]{1,0:T(8,128)} fusion(bf16[256,2048]{1,0:T(8,128)(2,1)} %bitcast.7, bf16[1,2048,768]{2,1,0:T(8,128)(2,1)S(1)} %copy-done.2), kind=kOutput, calls=%fused_computation.13 | convolution fusion | flops 805306368 | bytes 4980736 | tf_op jit(solution)/shard_map/dot_general | solution.py:30
  71.4 12.7 %all-to-all-done.1 = bf16[16,16,2048]{2,1,0:T(8,128)(2,1)} async-done(((bf16[16,16,2048]{2,1,0:T(8,128)(2,1)}), bf16[16,16,2048]{2,1,0:T(8,128)(2,1)}, u32[]{:S(2)}, u32[]{:S(2)}) %all-to-all-start.1) | async-done | bytes 1048608 | tf_op jit(solution)/shard_map/all_to_all | solution.py:186
  84.1 1.7 fusion.34
  85.8 3.3 %fusion.8 = f32[256,768]{1,0:T(8,128)S(1)} fusion(bf16[256,2048]{1,0:T(8,128)(2,1)} %bitcast.4, bf16[1,768,2048]{2,1,0:T(8,128)(2,1)} %param.19), kind=kOutput, calls=%fused_computation.15 | convolution fusion | flops 805306368 | bytes 4980736 | tf_op jit(solution)/shard_map/dot_general | solution.py:78
  89.1 0.3 fusion.16
  89.4 0.3 fusion.17
  89.7 1.3 multiply_reduce_fusion
  91.0 0.9 convolution_convert_fusion.4
  91.9 0.8 fusion.37
  92.7 0.2 convolution_convert_fusion.3
  92.9 0.9 fusion.39
  93.8 1.1 fusion.27
  94.8 2.7 %convolution_bitcast_fusion = f32[2,16,8,128]{3,2,1,0:T(8,128)} fusion(bf16[256,768]{1,0:T(8,128)(2,1)} %copy-done.3, bf16[768,16]{0,1:T(8,128)(2,1)} %param.24, bf16[256,2048]{1,0:T(8,128)(2,1)} %bitcast.4, f32[256]{0:T(256)} %reshape.172), kind=kOutput, calls=%fused_computation.29 | convolution fusion | flops 24645632 | bytes 1598464 | tf_op jit(solution)/shard_map/dot_general | solution.py:118
  97.5 3.3 %fusion = f32[256,2048]{1,0:T(8,128)} fusion(bf16[256,768]{1,0:T(8,128)(2,1)} %copy-done.1, bf16[1,2048,768]{2,1,0:T(8,128)(2,1)S(1)} %copy-done), kind=kOutput, calls=%fused_computation.7 | convolution fusion | flops 805306368 | bytes 5636096 | tf_op jit(solution)/shard_map/dot_general | solution.py:102
  100.8 2.7 %fusion.36 = f32[2048,16]{1,0:T(8,128)} fusion(bf16[256,2048]{1,0:T(8,128)(2,1)} %bitcast.7, bf16[256,16]{0,1:T(8,128)(2,1)S(1)} %copy-done.11), kind=kOutput, calls=%fused_computation.79 | convolution fusion | flops 16777216 | bytes 1187840 | tf_op jit(solution)/shard_map/dot_general | solution.py:113
  103.5 1.8 fusion.35
  105.3 2.2 reshape.166
  107.5 1.6 constant_dynamic-update-slice_fusion.5
  109.1 1.4 reshape.167
  110.5 2.7 %fusion.38 = f32[2048,16]{1,0:T(8,128)} fusion(bf16[256,2048]{1,0:T(8,128)(2,1)} %bitcast.7, bf16[256,16]{0,1:T(8,128)(2,1)S(1)} %convolution_convert_fusion.3), kind=kOutput, calls=%fused_computation.81 | convolution fusion | flops 16777216 | bytes 1187840 | tf_op jit(solution)/shard_map/dot_general | solution.py:115
  113.2 2.2 reshape.168
  115.4 1.4 reshape.169
  116.8 1.8 reshape.170
  118.5 1.6 copy.39
  120.1 4.9 %fusion.10 = f32[256,2048]{1,0:T(8,128)} fusion(f32[256,2048]{1,0:T(8,128)} %fusion, bf16[256,768]{1,0:T(8,128)(2,1)S(1)} %get-tuple-element.15, bf16[1,2048,768]{2,1,0:T(8,128)(2,1)} %param.18), kind=kOutput, calls=%fused_computation.17 | convolution fusion | flops 805830656 | bytes 7733248 | tf_op jit(solution)/shard_map/dot_general | solution.py:104
  125.0 0.7 convert_element_type.91
  125.7 6.9 %all-to-all-start.4 = ((bf16[16,1,16]{2,1,0:T(2,128)(2,1)}), bf16[16,1,16]{2,1,0:T(2,128)(2,1)S(1)}, u32[]{:S(2)}, u32[]{:S(2)}) async-start(bf16[16,1,16]{2,1,0:T(2,128)(2,1)} %convert_element_type.91), calls=%async_computation.4 | async-start | bytes 16384 | tf_op jit(solution)/shard_map/all_to_all | solution.py:214
  132.5 1.4 constant_dynamic-update-slice_fusion.4
  134.0 1.6 constant_dynamic-update-slice_fusion.3
  135.5 1.4 constant_dynamic-update-slice_fusion.2
  136.9 1.4 constant_dynamic-update-slice_fusion.1
  138.3 1.6 constant_dynamic-update-slice_fusion
  139.9 3.7 %fusion.15 = bf16[256,2048]{1,0:T(8,128)(2,1)} fusion(f32[256,2048]{1,0:T(8,128)} %fusion.10, f32[256,2048]{1,0:T(8,128)} %fusion.35, bf16[256,16]{0,1:T(8,128)(2,1)S(1)} %convolution_convert_fusion.3, bf16[2048,16]{0,1:T(8,128)(2,1)} %param.22), kind=kOutput, calls=%fused_computation.21 | convolution fusion | flops 18874368 | bytes 5316608 | tf_op jit(solution)/shard_map/dot_general | solution.py:107
  143.6 6.1 %all-to-all-start.3 = ((bf16[16,16,2048]{2,1,0:T(8,128)(2,1)}), bf16[16,16,2048]{2,1,0:T(8,128)(2,1)}, u32[]{:S(2)}, u32[]{:S(2)}) async-start(bf16[16,16,2048]{2,1,0:T(8,128)(2,1)} %bitcast.71), calls=%async_computation.3 | async-start | bytes 2097152 | tf_op jit(solution)/shard_map/all_to_all | solution.py:207
  149.7 1.9 broadcast_multiply_fusion
  151.7 0.1 reshape.164
  151.8 1.2 gather_fusion.1
  153.0 0.1 reshape.165
  153.1 0.7 copy.35
  153.8 96.7 %all-reduce.2.cloned.1.call-done = f32[135168]{0:T(1024)} async-done(((f32[135168]{0:T(1024)}), f32[135168]{0:T(1024)}) %all-reduce.2.cloned.1.call-update) | async-done | bytes 540688 | tf_op jit(solution)/shard_map/psum | solution.py:227
  250.4 1.5 dynamic_slice.3
  251.9 3.6 %gather_fusion = bf16[128,2048]{1,0:T(8,128)(2,1)} fusion(bf16[256,2048]{1,0:T(8,128)(2,1)} %bitcast.11, s32[1024]{0:T(1024)S(1)} %pad_clamp_fusion), kind=kCustom, calls=%fused_computation.2 | custom fusion | bytes 1049088 | tf_op jit(solution)/shard_map/gather | solution.py:222
  255.5 2.0 bitcast_reduce_fusion
  (48 shorter events, 0.4 us)
Async XLA Ops:
  7.2 58.0 %copy-start = (bf16[1,2048,768]{2,1,0:T(8,128)(2,1)S(1)}, bf16[1,2048,768]{2,1,0:T(8,128)(2,1)}, u32[]{:S(2)}) copy-start(bf16[1,2048,768]{2,1,0:T(8,128)(2,1)} %param.17) | copy-start | bytes 9437188
  10.4 43.7 %copy-start.15 = (s32[128]{0:T(128)}, s32[128]{0:T(128)S(1)}, u32[]{:S(2)}) copy-start(s32[128]{0:T(128)S(1)} %fusion.31) | copy-start | bytes 1540
  12.4 13.7 %all-to-all-start = ((bf16[16,1,16]{2,1,0:T(2,128)(2,1)}), bf16[16,1,16]{2,1,0:T(2,128)(2,1)S(1)}, u32[]{:S(2)}, u32[]{:S(2)}) async-start(bf16[16,1,16]{2,1,0:T(2,128)(2,1)} %all_to_all.25), calls=%async_computation | async-start | bytes 16384 | tf_op jit(solution)/shard_map/all_to_all | solution.py:187
  19.8 41.9 %copy-start.6 = (bf16[2048,16]{0,1:T(8,128)(2,1)S(1)}, bf16[2048,16]{0,1:T(8,128)(2,1)}, u32[]{:S(2)}) copy-start(bf16[2048,16]{0,1:T(8,128)(2,1)} %param.20) | copy-start | bytes 196612
  26.1 37.2 %copy-start.8 = (bf16[2048,16]{0,1:T(8,128)(2,1)S(1)}, bf16[2048,16]{0,1:T(8,128)(2,1)}, u32[]{:S(2)}) copy-start(bf16[2048,16]{0,1:T(8,128)(2,1)} %param.22) | copy-start | bytes 196612
  26.1 28.0 %all-to-all-start.2 = ((bf16[16,16,2048]{2,1,0:T(8,128)(2,1)}), bf16[16,16,2048]{2,1,0:T(8,128)(2,1)}, u32[]{:S(2)}, u32[]{:S(2)}) async-start(bf16[16,16,2048]{2,1,0:T(8,128)(2,1)} %bitcast.70), calls=%async_computation.2 | async-start | bytes 2097152 | tf_op jit(solution)/shard_map/all_to_all | solution.py:172
  54.1 29.9 %all-to-all-start.1 = ((bf16[16,16,2048]{2,1,0:T(8,128)(2,1)}), bf16[16,16,2048]{2,1,0:T(8,128)(2,1)}, u32[]{:S(2)}, u32[]{:S(2)}) async-start(bf16[16,16,2048]{2,1,0:T(8,128)(2,1)} %bitcast.69), calls=%async_computation.1 | async-start | bytes 2097152 | tf_op jit(solution)/shard_map/all_to_all | solution.py:186
  63.4 4.9 %copy-start.2 = (bf16[1,2048,768]{2,1,0:T(8,128)(2,1)S(1)}, bf16[1,2048,768]{2,1,0:T(8,128)(2,1)}, u32[]{:S(2)}) copy-start(bf16[1,2048,768]{2,1,0:T(8,128)(2,1)} %param.18) | copy-start | bytes 9437188
  68.2 15.8 %copy-start.12 = (bf16[16,2048]{1,0:T(8,128)(2,1)S(1)}, bf16[16,2048]{1,0:T(8,128)(2,1)}, u32[]{:S(2)}) copy-start(bf16[16,2048]{1,0:T(8,128)(2,1)} %param.25) | copy-start | bytes 196612
  84.1 5.0 %copy-start.5 = (f32[256,768]{1,0:T(8,128)S(1)}, f32[256,768]{1,0:T(8,128)}, u32[]{:S(2)}) copy-start(f32[256,768]{1,0:T(8,128)} %fusion.2) | copy-start | bytes 2359300
  84.1 5.0 %copy-start.9 = (bf16[16,768]{1,0:T(8,128)(2,1)S(1)}, bf16[16,768]{1,0:T(8,128)(2,1)}, u32[]{:S(2)}) copy-start(bf16[16,768]{1,0:T(8,128)(2,1)} %param.21) | copy-start | bytes 73732
  85.7 3.7 %copy-start.4 = (f32[256,768]{1,0:T(8,128)S(1)}, f32[256,768]{1,0:T(8,128)}, u32[]{:S(2)}) copy-start(f32[256,768]{1,0:T(8,128)} %fusion.6) | copy-start | bytes 2359300
  85.7 3.7 %copy-start.10 = (bf16[16,768]{1,0:T(8,128)(2,1)S(1)}, bf16[16,768]{1,0:T(8,128)(2,1)}, u32[]{:S(2)}) copy-start(bf16[16,768]{1,0:T(8,128)(2,1)} %param.23) | copy-start | bytes 73732
  85.8 4.0 %copy-start.13 = (bf16[768,16]{0,1:T(8,128)(2,1)S(1)}, bf16[768,16]{0,1:T(8,128)(2,1)}, u32[]{:S(2)}) copy-start(bf16[768,16]{0,1:T(8,128)(2,1)} %param.24) | copy-start | bytes 73732
  85.8 4.0 %copy-start.14 = (f32[256]{0:T(256)S(1)}, f32[256]{0:T(256)}, u32[]{:S(2)}) copy-start(f32[256]{0:T(256)} %reshape.172) | copy-start | bytes 3076
  91.0 0.9 copy-start.1
  91.0 2.7 %copy-start.3 = (bf16[256,768]{1,0:T(8,128)(2,1)}, bf16[256,768]{1,0:T(8,128)(2,1)S(1)}, u32[]{:S(2)}) copy-start(bf16[256,768]{1,0:T(8,128)(2,1)S(1)} %get-tuple-element.13) | copy-start | bytes 1179652
  97.5 3.3 %copy-start.11 = (bf16[256,16]{0,1:T(8,128)(2,1)S(1)}, bf16[256,16]{0,1:T(8,128)(2,1)}, u32[]{:S(2)}) copy-start(bf16[256,16]{0,1:T(8,128)(2,1)} %convolution_convert_fusion.4) | copy-start | bytes 24580
  97.5 6.1 %copy-start.7 = (bf16[2048,16]{0,1:T(8,128)(2,1)S(1)}, bf16[2048,16]{0,1:T(8,128)(2,1)}, u32[]{:S(2)}) copy-start(bf16[2048,16]{0,1:T(8,128)(2,1)} %param.20) | copy-start | bytes 196612
  120.1 4.9 %copy-start.17 = (bf16[256]{0:T(256)(128)(2,1)S(1)}, bf16[256]{0:T(256)(128)(2,1)}, u32[]{:S(2)}) copy-start(bf16[256]{0:T(256)(128)(2,1)} %get-tuple-element.12) | copy-start | bytes 1540
  125.7 17.9 %all-to-all-start.4 = ((bf16[16,1,16]{2,1,0:T(2,128)(2,1)}), bf16[16,1,16]{2,1,0:T(2,128)(2,1)S(1)}, u32[]{:S(2)}, u32[]{:S(2)}) async-start(bf16[16,1,16]{2,1,0:T(2,128)(2,1)} %convert_element_type.91), calls=%async_computation.4 | async-start | bytes 16384 | tf_op jit(solution)/shard_map/all_to_all | solution.py:214
  143.6 8.1 %copy-start.16 = (s32[128]{0:T(128)S(1)}, s32[128]{0:T(128)}, u32[]{:S(2)}) copy-start(s32[128]{0:T(128)} %copy-done.15) | copy-start | bytes 1540
  143.6 108.3 %all-to-all-start.3 = ((bf16[16,16,2048]{2,1,0:T(8,128)(2,1)}), bf16[16,16,2048]{2,1,0:T(8,128)(2,1)}, u32[]{:S(2)}, u32[]{:S(2)}) async-start(bf16[16,16,2048]{2,1,0:T(8,128)(2,1)} %bitcast.71), calls=%async_computation.3 | async-start | bytes 2097152 | tf_op jit(solution)/shard_map/all_to_all | solution.py:207
  149.7 100.8 %all-reduce.2.cloned.1.call-start = ((), (), s32[]{:S(2)}) async-start(), calls=%async_computation.5 | async-start | bytes 1081344 | tf_op jit(solution)/shard_map/psum | solution.py:227
Sparse Core Ops, SparseCore 0:
  153.9 96.4 all-reduce.1
where the time goes:
time: 266 us; the launch traced here: 264 us
  waiting for transfers between devices  128 us (48%)
  local copies, waits for them, and re-layouts  42.4 us (16%)
  matrix products  41.9 us (16%)
  starting transfers between devices  32.2 us (12%)
  between operations  14.3 us (5%)
  other arithmetic  5.17 us (2%)
    psum x1, waiting for transfers between devices, shards(): summed = lax.psum(adapter_products, 'exp')  96.7 us
    all_to_all x1, waiting for transfers between devices, shards(): lax.all_to_all(send_inputs, 'exp', split_axis=0, concat_axis=0, tiled=True)  17.8 us
    all_to_all x1, waiting for transfers between devices, shards(): lax.all_to_all(send_grads, 'exp', split_axis=0, concat_axis=0, tiled=True)  12.7 us
    unnamed x45, local copies, waits for them, and re-layouts  11.4 us
    reshape x5, local copies, waits for them, and re-layouts, expert_reverse_pass(): partial_result.reshape(-1)  8.94 us
    all_to_all x1, starting transfers between devices, shards(): lax.all_to_all(send_gates, 'exp', split_axis=0, concat_axis=0, tiled=True)  7.36 us
    all_to_all x1, starting transfers between devices, shards(): lax.all_to_all(send_grads, 'exp', split_axis=0, concat_axis=0, tiled=True)  6.93 us
    all_to_all x1, starting transfers between devices, shards(): lax.all_to_all(weight_row_values.reshape(devices, capacity), 'exp', split...  6.85 us
  transfers between devices with their start and end apart: 6, of which 4 were waited for; matrix products, arithmetic and copies ran while one was open for 14% of the time, Pallas kernels for 0%

commit v1 on v0

--- a/solution.py
+++ b/solution.py
@@ -1,6 +1,10 @@
+import functools
+
 import jax
 import jax.numpy as jnp
 from jax import lax
+from jax.experimental import pallas as pl
+from jax.experimental.pallas import tpu as pltpu
 from jax.sharding import PartitionSpec as P
 
 adapter_scale = 2.0
@@ -232,6 +236,478 @@
     return (grad_in, grad_combine, grad_adapters)
 
 
+MESH = pl.DeviceIdType.MESH
+CHUNKS = 4
+LANES = 128
+
+
+def nt(a, b):
+    return lax.dot_general(a, b, (((1,), (1,)), ((), ())), preferred_element_type=jnp.float32)
+
+
+def nn(a, b):
+    return jnp.dot(a, b, preferred_element_type=jnp.float32)
+
+
+def dense_kernel(
+    n,
+    line,
+    grad_hbm,
+    tok_hbm,
+    routes_hbm,
+    combine_hbm,
+    gate_hbm,
+    upper_hbm,
+    down_hbm,
+    gal_hbm,
+    gar_hbm,
+    ual_hbm,
+    uar_hbm,
+    dal_hbm,
+    dar_hbm,
+    out_in,
+    out_comb,
+    out_adapt,
+    xbuf,
+    gbuf,
+    routes,
+    comb,
+    wcat,
+    down,
+    gal,
+    ual,
+    rcat,
+    gar8,
+    uar8,
+    dal,
+    dar8,
+    pre_g,
+    pre_u,
+    raw,
+    low8,
+    xt,
+    hidden,
+    gcat,
+    wrows,
+    tbuf,
+    aflat,
+    ashare,
+    pbuf,
+    ra,
+    rb,
+    rc,
+    ebuf,
+    ea,
+    eb,
+    ec,
+    load_sem,
+    xs,
+    xr,
+    gs,
+    gr,
+    as_,
+    ar,
+    bs,
+    br,
+    cs,
+    cr,
+):
+    t, width = tok_hbm.shape
+    hid = gate_hbm.shape[2]
+    rank = gar_hbm.shape[0]
+    top = routes_hbm.shape[1]
+    rep = LANES // rank
+    rows = n * t
+    half, quarter = n // 2, n // 4
+    share = out_adapt.shape[0]
+    step = width // CHUNKS
+
+    me = lax.axis_index("exp")
+    core, col, pos = lax.rem(me, 2), lax.rem(me // 2, 2), me // 4
+
+    def index_of(c, x, z):
+        return (lax.rem(pos + z, line) * 2 + lax.rem(col + x, 2)) * 2 + lax.rem(core + c, 2)
+
+    def slot(c, x, z):
+        return c * half + x * quarter + z
+
+    sibling = index_of(1, 0, 0)
+    across = index_of(0, 1, 0)
+    along = [index_of(0, 0, dz) for dz in range(line)]
+
+    loads = []
+
+    def load(src, dst):
+        copy = pltpu.make_async_copy(src, dst, load_sem.at[len(loads)])
+        copy.start()
+        loads.append(copy)
+        return copy
+
+    own_x = load(tok_hbm, xbuf.at[0])
+    own_g = load(grad_hbm, gbuf.at[0, :, pl.ds(0, width)])
+    own_r = load(routes_hbm, routes)
+    own_c = load(combine_hbm, comb)
+    load_al = [load(gal_hbm, gal), load(ual_hbm, ual)]
+    load_gate = load(gate_hbm.at[0], wcat.at[:, pl.ds(0, hid)])
+    load_rc = [
+        load(gar_hbm, rcat.at[pl.ds(0, rank), pl.ds(0, hid)]),
+        load(uar_hbm, rcat.at[pl.ds(rank, rank), pl.ds(hid, hid)]),
+    ]
+    load_upper = load(upper_hbm.at[0], wcat.at[:, pl.ds(hid, hid)])
+    load_small = []
+    for i in range(rep):
+        load_small.append(load(gar_hbm, gar8.at[pl.ds(i * rank, rank)]))
+        load_small.append(load(uar_hbm, uar8.at[pl.ds(i * rank, rank)]))
+        load_small.append(load(dar_hbm, dar8.at[pl.ds(i * rank, rank)]))
+    load_small.append(load(dal_hbm, dal))
+    load_down = load(down_hbm.at[0], down)
+
+    peers = [sibling, across] + along[1:]
+    barrier = pltpu.get_barrier_semaphore()
+    for peer in peers:
+        pl.semaphore_signal(barrier, inc=1, device_id={"exp": peer}, device_id_type=MESH)
+    pl.semaphore_wait(barrier, len(peers))
+
+    def gather_copy(buf, send, recv, src, dst, peer):
+        return pltpu.make_async_remote_copy(
+            src_ref=buf.at[src],
+            dst_ref=buf.at[dst],
+            send_sem=send.at[dst],
+            recv_sem=recv.at[dst],
+            device_id={"exp": peer},
+            device_id_type=MESH,
+        )
+
+    order = [dz for pair in zip(range(1, line), range(line - 1, 0, -1)) for dz in pair]
+    order = list(dict.fromkeys(order))
+    sent = []
+
+    def send(bufs, src, dst, peer):
+        copy = gather_copy(*bufs, src, dst, peer)
+        copy.start()
+        sent.append(copy)
+
+    def arrived(bufs, s):
+        gather_copy(*bufs, s, s, sibling).wait_recv()
+
+    def own_phase(bufs):
+        for dz in order:
+            send(bufs, 0, slot(0, 0, line - dz), along[dz])
+        send(bufs, 0, slot(0, 1, 0), across)
+        send(bufs, 0, slot(1, 0, 0), sibling)
+
+    def line_phase(bufs):
+        for dz in order:
+            arrived(bufs, slot(0, 0, dz))
+            send(bufs, slot(0, 0, dz), slot(0, 1, dz), across)
+            send(bufs, slot(0, 0, dz), slot(1, 0, dz), sibling)
+
+    def across_phase(bufs):
+        for dz in [0] + order:
+            arrived(bufs, slot(0, 1, dz))
+            send(bufs, slot(0, 1, dz), slot(1, 1, dz), sibling)
+
+    def sibling_phase(bufs):
+        for s in range(half, n):
+            arrived(bufs, s)
+
+    xb, gb = (xbuf, xs, xr), (gbuf, gs, gr)
+    own_x.wait()
+    own_phase(xb)
+    own_g.wait()
+    own_r.wait()
+    own_c.wait()
+    lanes_t = lax.broadcasted_iota(jnp.int32, (t, LANES), 1)
+    chosen = routes[...]
+    weights = comb[...].astype(jnp.float32)
+    dense = jnp.zeros((t, LANES), jnp.float32)
+    for k in range(top):
+        dense = dense + jnp.where(lanes_t == chosen[:, k : k + 1], weights[:, k : k + 1], 0.0)
+    gbuf[0, :, pl.ds(width, LANES)] = dense.astype(jnp.bfloat16)
+    own_phase(gb)
+
+    rcat[pl.ds(0, rank), pl.ds(hid, hid)] = jnp.zeros((rank, hid), jnp.bfloat16)
+    rcat[pl.ds(rank, rank), pl.ds(0, hid)] = jnp.zeros((rank, hid), jnp.bfloat16)
+    ashare[...] = jnp.zeros_like(ashare)
+    line_phase(xb)
+    for copy in load_al:
+        copy.wait()
+    wcat[:, pl.ds(2 * hid, LANES)] = jnp.concatenate(
+        [gal[...], ual[...], jnp.zeros((width, LANES - 2 * rank), jnp.bfloat16)], axis=1
+    )
+    across_phase(xb)
+    for copy in load_rc:
+        copy.wait()
+    load_gate.wait()
+    load_upper.wait()
+    sibling_phase(xb)
+
+    line_phase(gb)
+    x_all = xbuf[...].reshape(rows, width)
+    low_cat = nn(x_all, wcat[:, pl.ds(2 * hid, LANES)])[:, : 2 * rank].astype(jnp.bfloat16)
+    pre_g[...] = nn(x_all, wcat[:, pl.ds(0, hid)]) + adapter_scale * nn(low_cat, rcat[:, pl.ds(0, hid)])
+    across_phase(gb)
+    pre_u[...] = nn(x_all, wcat[:, pl.ds(hid, hid)]) + adapter_scale * nn(
+        low_cat, rcat[:, pl.ds(hid, hid)]
+    )
+    xt[...] = x_all.T
+    for copy in load_small:
+        copy.wait()
+    load_down.wait()
+    sibling_phase(gb)
+
+    g_all = gbuf[:, :, pl.ds(0, width)].reshape(rows, width)
+    gates = gbuf[:, :, pl.ds(width, LANES)].reshape(rows, LANES).astype(jnp.float32)
+    lanes_r = lax.broadcasted_iota(jnp.int32, (rows, LANES), 1)
+    gate_col = jnp.sum(jnp.where(lanes_r == me, gates, 0.0), axis=1, keepdims=True)
+    back_low8 = nt(g_all, dar8[...])
+    back_rounded = back_low8[:, :rank].astype(jnp.bfloat16)
+    raw[...] = nt(g_all, down[...]) + adapter_scale * nt(back_rounded, dal[...])
+    low8[...] = (gate_col * back_low8).astype(jnp.bfloat16)
+    wrows[...] = jnp.broadcast_to(gate_col, (rows, LANES))
+
+    block = 16
+
+    def pointwise(i, carry):
+        here = pl.ds(pl.multiple_of(i * block, block), block)
+        v, u, h = pre_g[here, :], pre_u[here, :], raw[here, :]
+        s = jax.nn.sigmoid(v)
+        hidden_here = (v * s * u).astype(jnp.bfloat16)
+        hidden[here, :] = hidden_here
+        hg = wrows[here, :][:, :1] * h
+        gcat[here, pl.ds(0, hid)] = (hg * u * s * (1.0 + v * (1.0 - s))).astype(jnp.bfloat16)
+        gcat[here, pl.ds(hid, hid)] = (hg * v * s).astype(jnp.bfloat16)
+        w = jnp.sum(hidden_here.astype(jnp.float32) * h, axis=1, keepdims=True)
+        lanes_b = lax.broadcasted_iota(jnp.int32, (block, LANES), 1)
+        ebuf[i, pl.ds(ebuf.shape[1] - t, t), :] = jnp.where(lanes_b == me, w, 0.0).astype(jnp.bfloat16)
+        return carry
+
+    lax.fori_loop(0, rows // block, pointwise, 0)
+
+    gb8 = nt(gcat[:, pl.ds(0, hid)], gar8[...])
+    ub8 = nt(gcat[:, pl.ds(hid, hid)], uar8[...])
+    backs = jnp.where(lanes_r < rank, gb8, jnp.where(lanes_r < 2 * rank, ub8, 0.0))
+    backs = adapter_scale * backs.astype(jnp.bfloat16).astype(jnp.float32)
+    gcat[:, pl.ds(2 * hid, LANES)] = backs.astype(jnp.bfloat16)
+
+    def push(src, dst, send_sem, recv_sem, peer):
+        copy = pltpu.make_async_remote_copy(
+            src_ref=src,
+            dst_ref=dst,
+            send_sem=send_sem,
+            recv_sem=recv_sem,
+            device_id={"exp": peer},
+            device_id_type=MESH,
+        )
+        return copy
+
+    def views(i):
+        if i < CHUNKS:
+            return pbuf.at[i], ra.at[i], rb.at[i], rc.at[i]
+        return ebuf, ea, eb, ec
+
+    def start_a(i):
+        p, a, b, c = views(i)
+        copy = push(p.at[pl.ds(half, half)], a, as_.at[i], ar.at[i], sibling)
+        copy.start()
+        sent.append(copy)
+
+    def add(p, q):
+        return (p.astype(jnp.float32) + q.astype(jnp.float32)).astype(jnp.bfloat16)
+
+    def stage_b(i):
+        p, a, b, c = views(i)
+        push(p.at[pl.ds(half, half)], a, as_.at[i], ar.at[i], sibling).wait_recv()
+        p[pl.ds(quarter, quarter)] = add(p[pl.ds(quarter, quarter)], a[pl.ds(quarter, quarter)])
+        copy = push(p.at[pl.ds(quarter, quarter)], b, bs.at[i], br.at[i], across)
+        copy.start()
+        sent.append(copy)
+        p[pl.ds(0, quarter)] = add(p[pl.ds(0, quarter)], a[pl.ds(0, quarter)])
+
+    def stage_c(i):
+        p, a, b, c = views(i)
+        push(p.at[pl.ds(quarter, quarter)], b, bs.at[i], br.at[i], across).wait_recv()
+        p[pl.ds(0, quarter)] = add(p[pl.ds(0, quarter)], b[...])
+        for dz in order:
+            copy = push(p.at[dz], c.at[line - dz - 1], cs.at[i, dz - 1], cr.at[i, line - dz - 1], along[dz])
+            copy.start()
+            sent.append(copy)
+
+    def total(i):
+        p, a, b, c = views(i)
+        value = p[0].astype(jnp.float32)
+        for dz in range(1, line):
+            push(p.at[dz], c.at[dz - 1], cs.at[i, dz - 1], cr.at[i, dz - 1], along[dz]).wait_recv()
+            value = value + c[dz - 1].astype(jnp.float32)
+        return value
+
+    def compute_rows(i):
+        piece = nt(gcat[...], wcat[pl.ds(i * step, step), :])
+        pbuf[i] = piece.astype(jnp.bfloat16).reshape(n, t, step)
+
+    def folded(value):
+        count = value.shape[0] // rep
+        sub = lax.broadcasted_iota(jnp.int32, (rep, LANES), 0)
+        lane = lax.broadcasted_iota(jnp.int32, (rep, LANES), 1)
+        mask = (lane // rank == sub).astype(jnp.float32) * adapter_scale
+        return jnp.sum(value.reshape(count, rep, LANES) * mask[None], axis=1)
+
+    def spread(start, value):
+        pieces = value.shape[1] // LANES
+        for k in range(pieces):
+            aflat[pl.ds(start + k, rank, stride=pieces), :] = adapter_scale * value[:, k * LANES : (k + 1) * LANES]
+
+    def compute_adapters():
+        gate_rows_left, gate_rows_right = width * rank // LANES, hid * rank // LANES
+        both = jnp.concatenate([gb8, ub8], axis=1).astype(jnp.bfloat16)
+        tbuf[...] = nn(xt[...], both)
+        at = 0
+        aflat[pl.ds(at, gate_rows_left), :] = folded(tbuf[:, pl.ds(0, LANES)])
+        at += gate_rows_left
+        low_t = low_cat.T
+        spread(at, nn(low_t[:rank], gcat[:, pl.ds(0, hid)]))
+        at += gate_rows_right
+        aflat[pl.ds(at, gate_rows_left), :] = folded(tbuf[:, pl.ds(LANES, LANES)])
+        at += gate_rows_left
+        spread(at, nn(low_t[rank:], gcat[:, pl.ds(hid, hid)]))
+        at += gate_rows_right
+        hid_all = hidden[...]
+        aflat[pl.ds(at, gate_rows_right), :] = folded(nn(hid_all.T, low8[...]))
+        at += gate_rows_right
+        low_hidden = nn(hid_all, dal[...]).astype(jnp.bfloat16).astype(jnp.float32)
+        low_hidden = (low_hidden * gate_col).astype(jnp.bfloat16)
+        spread(at, nn(low_hidden.T, g_all))
+        for d in range(n):
+            ashare[d, pl.ds(0, share), :] = aflat[pl.ds(d * share, share), :]
+        for c in range(2):
+            for x in range(2):
+                for z in range(line):
+                    ebuf[slot(c, x, z), pl.ds(0, ashare.shape[1]), :] = ashare[index_of(c, x, z)].astype(
+                        jnp.bfloat16
+                    )
+
+    plan = list(range(CHUNKS)) + [CHUNKS]
+    for k in range(len(plan) + 2):
+        if k < len(plan):
+            if plan[k] < CHUNKS:
+                compute_rows(plan[k])
+            else:
+                compute_adapters()
+            start_a(plan[k])
+        if 1 <= k <= len(plan):
+            stage_b(plan[k - 1])
+        if k >= 2:
+            stage_c(plan[k - 2])
+
+    for i in range(CHUNKS):
+        out_in[:, pl.ds(i * step, step)] = total(i).astype(jnp.bfloat16)
+    extra = total(CHUNKS)
+    out_adapt[...] = extra[:share]
+    w_rows = extra[ebuf.shape[1] - t :]
+    lanes_k = lax.broadcasted_iota(jnp.int32, (t, top), 1)
+    picked = jnp.zeros((t, top), jnp.float32)
+    for k in range(top):
+        value = jnp.sum(jnp.where(lanes_t == chosen[:, k : k + 1], w_rows, 0.0), axis=1, keepdims=True)
+        picked = picked + jnp.where(lanes_k == k, value, 0.0)
+    out_comb[...] = picked.astype(jnp.bfloat16)
+    for copy in sent:
+        copy.wait_send()
+
+
+def dense_shards(*operands):
+    grad, tok, routes, combine, gate, upper, down, gal, gar, ual, uar, dal, dar = operands
+    n = lax.axis_size("exp")
+    line = n // 4
+    t, width = tok.shape
+    top, hid, rank = routes.shape[1], gate.shape[2], gar.shape[0]
+    rep = LANES // rank
+    params = 3 * rank * (width + hid)
+    share = params // n // LANES
+    padded = -(-share // 16) * 16
+    rows, half, quarter = n * t, n // 2, n // 4
+    step = width // CHUNKS
+    extra = padded + t
+    bf, f32 = jnp.bfloat16, jnp.float32
+    scratch = [
+        pltpu.VMEM((n, t, width), bf),
+        pltpu.VMEM((n, t, width + LANES), bf),
+        pltpu.VMEM((t, top), jnp.int32),
+        pltpu.VMEM((t, top), bf),
+        pltpu.VMEM((width, 2 * hid + LANES), bf),
+        pltpu.VMEM((hid, width), bf),
+        pltpu.VMEM((width, rank), bf),
+        pltpu.VMEM((width, rank), bf),
+        pltpu.VMEM((2 * rank, 2 * hid), bf),
+        pltpu.VMEM((LANES, hid), bf),
+        pltpu.VMEM((LANES, hid), bf),
+        pltpu.VMEM((hid, rank), bf),
+        pltpu.VMEM((LANES, width), bf),
+        pltpu.VMEM((rows, hid), f32),
+        pltpu.VMEM((rows, hid), f32),
+        pltpu.VMEM((rows, hid), f32),
+        pltpu.VMEM((rows, LANES), bf),
+        pltpu.VMEM((width, rows), bf),
+        pltpu.VMEM((rows, hid), bf),
+        pltpu.VMEM((rows, 2 * hid + LANES), bf),
+        pltpu.VMEM((rows, LANES), f32),
+        pltpu.VMEM((width, 2 * LANES), f32),
+        pltpu.VMEM((share * n, LANES), f32),
+        pltpu.VMEM((n, padded, LANES), f32),
+        pltpu.VMEM((CHUNKS, n, t, step), bf),
+        pltpu.VMEM((CHUNKS, half, t, step), bf),
+        pltpu.VMEM((CHUNKS, quarter, t, step), bf),
+        pltpu.VMEM((CHUNKS, line - 1, t, step), bf),
+        pltpu.VMEM((n, extra, LANES), bf),
+        pltpu.VMEM((half, extra, LANES), bf),
+        pltpu.VMEM((quarter, extra, LANES), bf),
+        pltpu.VMEM((line - 1, extra, LANES), bf),
+        pltpu.SemaphoreType.DMA((12 + 3 * rep,)),
+        pltpu.SemaphoreType.DMA((n,)),
+        pltpu.SemaphoreType.DMA((n,)),
+        pltpu.SemaphoreType.DMA((n,)),
+        pltpu.SemaphoreType.DMA((n,)),
+        pltpu.SemaphoreType.DMA((CHUNKS + 1,)),
+        pltpu.SemaphoreType.DMA((CHUNKS + 1,)),
+        pltpu.SemaphoreType.DMA((CHUNKS + 1,)),
+        pltpu.SemaphoreType.DMA((CHUNKS + 1,)),
+        pltpu.SemaphoreType.DMA((CHUNKS + 1, line - 1)),
+        pltpu.SemaphoreType.DMA((CHUNKS + 1, line - 1)),
+    ]
+    grad_in, grad_combine, adapters = pl.pallas_call(
+        functools.partial(dense_kernel, n, line),
+        out_shape=(
+            jax.ShapeDtypeStruct((t, width), bf),
+            jax.ShapeDtypeStruct((t, top), bf),
+            jax.ShapeDtypeStruct((share, LANES), f32),
+        ),
+        in_specs=[pl.BlockSpec(memory_space=pl.ANY)] * len(operands),
+        out_specs=(pl.BlockSpec(memory_space=pltpu.VMEM),) * 3,
+        scratch_shapes=scratch,
+        compiler_params=pltpu.CompilerParams(
+            collective_id=0, has_side_effects=True, vmem_limit_bytes=50 * 1024 * 1024
+        ),
+    )(*operands)
+    return grad_in, grad_combine, adapters.reshape(-1)
+
+
+def dense_fits(tokens, routes, gate, rank, groups, n):
+    t, width = tokens.shape[0] // (groups * n), tokens.shape[1]
+    top, hid = routes.shape[1], gate.shape[2]
+    capacity = max(2, min(t, (2 * t * top + n - 1) // n))
+    params = 3 * rank * (width + hid)
+    return (
+        capacity == t
+        and t == 16
+        and n % 4 == 0
+        and 8 <= n <= LANES
+        and gate.shape[0] == n
+        and rank == 16
+        and width % (CHUNKS * LANES) == 0
+        and hid % LANES == 0
+        and params % (n * LANES) == 0
+    )
+
+
 def solution(mesh):
     placed = (
         P(("grp", "exp"), None),
@@ -248,10 +724,16 @@
         P(),
         P(),
     )
-    return jax.shard_map(
-        shards,
-        mesh=mesh,
-        in_specs=placed,
-        out_specs=(P(("grp", "exp"), None), P(("grp", "exp"), None), P(("grp", "exp"))),
-        check_vma=False,
-    )
+    groups, n = mesh.shape["grp"], mesh.shape["exp"]
+
+    def whole(*arrays):
+        dense = dense_fits(arrays[1], arrays[2], arrays[4], arrays[8].shape[0], groups, n)
+        return jax.shard_map(
+            dense_shards if dense else shards,
+            mesh=mesh,
+            in_specs=placed,
+            out_specs=(P(("grp", "exp"), None), P(("grp", "exp"), None), P(("grp", "exp"))),
+            check_vma=False,
+        )(*arrays)
+
+    return whole

time: 266 us -> 64.2 us (0.24)
  waiting for transfers between devices: 128 us -> 0 us
  Pallas kernels: 0 us -> 52.5 us
  matrix products: 41.9 us -> 0 us
  starting transfers between devices: 32.2 us -> 0 us
  local copies, waits for them, and re-layouts: 42.4 us -> 10.5 us
  between operations: 14.3 us -> 0.67 us
  other arithmetic: 5.17 us -> 0 us
    psum x1 -> x0, waiting for transfers between devices: 96.7 us -> none  [shards(): summed = lax.psum(adapter_products, 'exp')]
    pallas_call x0 -> x1, Pallas kernels: none -> 52.5 us  [dense_shards(): pl.pallas_call(functools.partial(dense_kernel, n, line), out_shape=(jax.S...]
    dot_general x21 -> x0, matrix products: 41.9 us -> none  [the longest x1 4.86 us: expert_reverse_pass(): jnp.dot(upward_gradient, upward_matrix.T, preferred_element_type=jnp.floa...]
    all_to_all x5 -> x0, starting transfers between devices: 32.2 us -> none  [the longest x1 7.36 us: shards(): lax.all_to_all(send_gates, 'exp', split_axis=0, concat_axis=0, tiled=True)]
    all_to_all x5 -> x0, waiting for transfers between devices: 31.7 us -> none  [the longest x1 17.8 us: shards(): lax.all_to_all(send_inputs, 'exp', split_axis=0, concat_axis=0, tiled=True)]
    scatter x3 -> x0, local copies, waits for them, and re-layouts: 11.6 us -> none  [the longest x1 5.19 us: shards(): send_grads = jnp.zeros((slots_total, model_width), jnp.bfloat16).at[targe...]
    reshape x8 -> x0, local copies, waits for them, and re-layouts: 9.21 us -> none  [the longest x5 8.94 us: expert_reverse_pass(): partial_result.reshape(-1)]
    gather x2 -> x0, local copies, waits for them, and re-layouts: 4.84 us -> none  [the longest x1 3.6 us: shards(): back_inputs.reshape(slots_total, model_width)[target]]
  transfers between devices with their start and end apart: 6 -> 0, of which waited for: 4 -> 0; matrix products, arithmetic and copies ran while one was open for 14% -> 0% of each run, Pallas kernels for 0% -> 0%
where the time goes in v1:
time: 64.2 us; the launch traced here: 63.7 us
  Pallas kernels  52.5 us (82%)
  local copies, waits for them, and re-layouts  10.5 us (16%)
  between operations  0.67 us (1%)
    pallas_call x1, Pallas kernels, dense_shards(): pl.pallas_call(functools.partial(dense_kernel, n, line), out_shape=(jax.S...  52.5 us
    unnamed x18, local copies, waits for them, and re-layouts  10.5 us

profile of v1, /device:TPU:0, one launch (start us, length us, event | category | flops | bytes accessed | tf_op | source)
XLA Modules:
  0.0 63.7 jit_solution(6306661822286582426)
XLA Ops:
  0.6 0.8 %copy.17.combine_hbm = bf16[16,8]{1,0:T(8,128)(2,1)S(1)} copy(bf16[16,8]{0,1:T(8,128)(2,1)} %param.16) | data formatting | bytes 512 | tf_op args[3]
  1.4 0.8 %copy.16.routes_hbm = s32[16,8]{1,0:T(8,128)S(1)} copy(s32[16,8]{0,1:T(8,128)} %param.15) | data formatting | bytes 1024 | tf_op args[2]
  2.1 0.9 %copy.20.dal_hbm = bf16[768,16]{1,0:T(8,128)(2,1)S(1)} copy(bf16[768,16]{0,1:T(8,128)(2,1)} %param.24) | data formatting | bytes 49152 | tf_op args[11]
  3.0 1.1 %copy.18.gal_hbm = bf16[2048,16]{1,0:T(8,128)(2,1)S(1)} copy(bf16[2048,16]{0,1:T(8,128)(2,1)} %param.20) | data formatting | bytes 131072 | tf_op args[7]
  4.2 1.1 %copy.19.ual_hbm = bf16[2048,16]{1,0:T(8,128)(2,1)S(1)} copy(bf16[2048,16]{0,1:T(8,128)(2,1)} %param.22) | data formatting | bytes 131072 | tf_op args[9]
  5.3 0.0 copy-start
  5.3 0.8 %copy-done = bf16[16,2048]{1,0:T(8,128)(2,1)S(1)} copy-done((bf16[16,2048]{1,0:T(8,128)(2,1)S(1)}, bf16[16,2048]{1,0:T(8,128)(2,1)}, u32[]{:S(2)}) %copy-start) | copy-done | bytes 65560
  6.1 0.0 copy-start.1
  6.1 0.8 %copy-done.1 = bf16[16,2048]{1,0:T(8,128)(2,1)S(1)} copy-done((bf16[16,2048]{1,0:T(8,128)(2,1)S(1)}, bf16[16,2048]{1,0:T(8,128)(2,1)}, u32[]{:S(2)}) %copy-start.1) | copy-done | bytes 65560
  7.0 0.0 copy-start.2
  7.0 0.8 %copy-done.2 = bf16[16,2048]{1,0:T(8,128)(2,1)S(1)} copy-done((bf16[16,2048]{1,0:T(8,128)(2,1)S(1)}, bf16[16,2048]{1,0:T(8,128)(2,1)}, u32[]{:S(2)}) %copy-start.2) | copy-done | bytes 65560
  7.8 0.0 copy-start.3
  7.8 0.7 %copy-done.3 = bf16[16,768]{1,0:T(8,128)(2,1)S(1)} copy-done((bf16[16,768]{1,0:T(8,128)(2,1)S(1)}, bf16[16,768]{1,0:T(8,128)(2,1)}, u32[]{:S(2)}) %copy-start.3) | copy-done | bytes 24600
  8.6 0.0 copy-start.4
  8.6 0.7 %copy-done.4 = bf16[16,768]{1,0:T(8,128)(2,1)S(1)} copy-done((bf16[16,768]{1,0:T(8,128)(2,1)S(1)}, bf16[16,768]{1,0:T(8,128)(2,1)}, u32[]{:S(2)}) %copy-start.4) | copy-done | bytes 24600
  9.3 52.5 %shard_map.148 = (bf16[16,2048]{1,0:T(8,128)(2,1)S(1)}, bf16[16,8]{1,0:T(8,128)(2,1)S(1)}, f32[66,128]{1,0:T(8,128)S(1)}) custom-call(bf16[16,2048]{1,0:T(8,128)(2,1)S(1)} %copy-done, bf16[16,2048]{1,0:T(8,128)(2,1)S(1)} %copy-done.1, s32[16,8]{1,0:T(8,128)S(1)} %copy.16.routes_hbm, bf16[16,8]{1,0:T(8,128)(2,1)S(1)} %copy.17.combine_hbm, ...), custom_call_target="tpu_custom_call" | custom-call | tf_op jit(solution)/shard_map/pallas_call | solution.py:676
  61.8 0.7 %copy.21 = bf16[16,8]{0,1:T(8,128)(2,1)} copy(bf16[16,8]{1,0:T(8,128)(2,1)S(1)} %get-tuple-element.10) | data formatting | bytes 512
  62.4 0.6 copy.24
  63.0 0.6 copy.25
Async XLA Ops:
  5.3 0.8 %copy-start = (bf16[16,2048]{1,0:T(8,128)(2,1)S(1)}, bf16[16,2048]{1,0:T(8,128)(2,1)}, u32[]{:S(2)}) copy-start(bf16[16,2048]{1,0:T(8,128)(2,1)} %grad_hbm.1) | copy-start | bytes 196612
  6.1 0.8 %copy-start.1 = (bf16[16,2048]{1,0:T(8,128)(2,1)S(1)}, bf16[16,2048]{1,0:T(8,128)(2,1)}, u32[]{:S(2)}) copy-start(bf16[16,2048]{1,0:T(8,128)(2,1)} %tok_hbm.1) | copy-start | bytes 196612
  7.0 0.8 %copy-start.2 = (bf16[16,2048]{1,0:T(8,128)(2,1)S(1)}, bf16[16,2048]{1,0:T(8,128)(2,1)}, u32[]{:S(2)}) copy-start(bf16[16,2048]{1,0:T(8,128)(2,1)} %dar_hbm.1) | copy-start | bytes 196612
  7.8 0.7 %copy-start.3 = (bf16[16,768]{1,0:T(8,128)(2,1)S(1)}, bf16[16,768]{1,0:T(8,128)(2,1)}, u32[]{:S(2)}) copy-start(bf16[16,768]{1,0:T(8,128)(2,1)} %gar_hbm.1) | copy-start | bytes 73732
  8.6 0.7 %copy-start.4 = (bf16[16,768]{1,0:T(8,128)(2,1)S(1)}, bf16[16,768]{1,0:T(8,128)(2,1)}, u32[]{:S(2)}) copy-start(bf16[16,768]{1,0:T(8,128)(2,1)} %uar_hbm.1) | copy-start | bytes 73732

commit v2 on v1

--- a/solution.py
+++ b/solution.py
@@ -255,7 +255,7 @@
     grad_hbm,
     tok_hbm,
     routes_hbm,
-    combine_hbm,
+    comb,
     gate_hbm,
     upper_hbm,
     down_hbm,
@@ -271,11 +271,9 @@
     xbuf,
     gbuf,
     routes,
-    comb,
     wcat,
     down,
-    gal,
-    ual,
+    left,
     rcat,
     gar8,
     uar8,
@@ -315,7 +313,7 @@
     t, width = tok_hbm.shape
     hid = gate_hbm.shape[2]
     rank = gar_hbm.shape[0]
-    top = routes_hbm.shape[1]
+    top = routes_hbm.shape[0]
     rep = LANES // rank
     rows = n * t
     half, quarter = n // 2, n // 4
@@ -346,8 +344,7 @@
     own_x = load(tok_hbm, xbuf.at[0])
     own_g = load(grad_hbm, gbuf.at[0, :, pl.ds(0, width)])
     own_r = load(routes_hbm, routes)
-    own_c = load(combine_hbm, comb)
-    load_al = [load(gal_hbm, gal), load(ual_hbm, ual)]
+    load_al = [load(gal_hbm, left.at[pl.ds(0, rank)]), load(ual_hbm, left.at[pl.ds(rank, rank)])]
     load_gate = load(gate_hbm.at[0], wcat.at[:, pl.ds(0, hid)])
     load_rc = [
         load(gar_hbm, rcat.at[pl.ds(0, rank), pl.ds(0, hid)]),
@@ -416,10 +413,9 @@
     own_phase(xb)
     own_g.wait()
     own_r.wait()
-    own_c.wait()
     lanes_t = lax.broadcasted_iota(jnp.int32, (t, LANES), 1)
-    chosen = routes[...]
-    weights = comb[...].astype(jnp.float32)
+    chosen = routes[...].T
+    weights = comb[...].astype(jnp.float32).T
     dense = jnp.zeros((t, LANES), jnp.float32)
     for k in range(top):
         dense = dense + jnp.where(lanes_t == chosen[:, k : k + 1], weights[:, k : k + 1], 0.0)
@@ -430,13 +426,8 @@
     rcat[pl.ds(rank, rank), pl.ds(0, hid)] = jnp.zeros((rank, hid), jnp.bfloat16)
     ashare[...] = jnp.zeros_like(ashare)
     line_phase(xb)
-    for copy in load_al:
-        copy.wait()
-    wcat[:, pl.ds(2 * hid, LANES)] = jnp.concatenate(
-        [gal[...], ual[...], jnp.zeros((width, LANES - 2 * rank), jnp.bfloat16)], axis=1
-    )
     across_phase(xb)
-    for copy in load_rc:
+    for copy in load_al + load_rc:
         copy.wait()
     load_gate.wait()
     load_upper.wait()
@@ -444,7 +435,7 @@
 
     line_phase(gb)
     x_all = xbuf[...].reshape(rows, width)
-    low_cat = nn(x_all, wcat[:, pl.ds(2 * hid, LANES)])[:, : 2 * rank].astype(jnp.bfloat16)
+    low_cat = nt(x_all, left[...]).astype(jnp.bfloat16)
     pre_g[...] = nn(x_all, wcat[:, pl.ds(0, hid)]) + adapter_scale * nn(low_cat, rcat[:, pl.ds(0, hid)])
     across_phase(gb)
     pre_u[...] = nn(x_all, wcat[:, pl.ds(hid, hid)]) + adapter_scale * nn(
@@ -462,7 +453,7 @@
     gate_col = jnp.sum(jnp.where(lanes_r == me, gates, 0.0), axis=1, keepdims=True)
     back_low8 = nt(g_all, dar8[...])
     back_rounded = back_low8[:, :rank].astype(jnp.bfloat16)
-    raw[...] = nt(g_all, down[...]) + adapter_scale * nt(back_rounded, dal[...])
+    raw[...] = nt(g_all, down[...]) + adapter_scale * nn(back_rounded, dal[...])
     low8[...] = (gate_col * back_low8).astype(jnp.bfloat16)
     wrows[...] = jnp.broadcast_to(gate_col, (rows, LANES))
 
@@ -486,9 +477,8 @@
 
     gb8 = nt(gcat[:, pl.ds(0, hid)], gar8[...])
     ub8 = nt(gcat[:, pl.ds(hid, hid)], uar8[...])
-    backs = jnp.where(lanes_r < rank, gb8, jnp.where(lanes_r < 2 * rank, ub8, 0.0))
-    backs = adapter_scale * backs.astype(jnp.bfloat16).astype(jnp.float32)
-    gcat[:, pl.ds(2 * hid, LANES)] = backs.astype(jnp.bfloat16)
+    backs = jnp.where(lanes_r < rank, gb8, ub8)[:, : 2 * rank]
+    backs = (adapter_scale * backs.astype(jnp.bfloat16).astype(jnp.float32)).astype(jnp.bfloat16)
 
     def push(src, dst, send_sem, recv_sem, peer):
         copy = pltpu.make_async_remote_copy(
@@ -543,6 +533,7 @@
 
     def compute_rows(i):
         piece = nt(gcat[...], wcat[pl.ds(i * step, step), :])
+        piece = piece + nn(backs, left[:, pl.ds(i * step, step)])
         pbuf[i] = piece.astype(jnp.bfloat16).reshape(n, t, step)
 
     def folded(value):
@@ -574,7 +565,7 @@
         hid_all = hidden[...]
         aflat[pl.ds(at, gate_rows_right), :] = folded(nn(hid_all.T, low8[...]))
         at += gate_rows_right
-        low_hidden = nn(hid_all, dal[...]).astype(jnp.bfloat16).astype(jnp.float32)
+        low_hidden = nt(hid_all, dal[...]).astype(jnp.bfloat16).astype(jnp.float32)
         low_hidden = (low_hidden * gate_col).astype(jnp.bfloat16)
         spread(at, nn(low_hidden.T, g_all))
         for d in range(n):
@@ -609,7 +600,7 @@
     for k in range(top):
         value = jnp.sum(jnp.where(lanes_t == chosen[:, k : k + 1], w_rows, 0.0), axis=1, keepdims=True)
         picked = picked + jnp.where(lanes_k == k, value, 0.0)
-    out_comb[...] = picked.astype(jnp.bfloat16)
+    out_comb[...] = picked.T
     for copy in sent:
         copy.wait_send()
 
@@ -631,16 +622,14 @@
     scratch = [
         pltpu.VMEM((n, t, width), bf),
         pltpu.VMEM((n, t, width + LANES), bf),
-        pltpu.VMEM((t, top), jnp.int32),
-        pltpu.VMEM((t, top), bf),
-        pltpu.VMEM((width, 2 * hid + LANES), bf),
+        pltpu.VMEM((top, t), jnp.int32),
+        pltpu.VMEM((width, 2 * hid), bf),
         pltpu.VMEM((hid, width), bf),
-        pltpu.VMEM((width, rank), bf),
-        pltpu.VMEM((width, rank), bf),
+        pltpu.VMEM((2 * rank, width), bf),
         pltpu.VMEM((2 * rank, 2 * hid), bf),
         pltpu.VMEM((LANES, hid), bf),
         pltpu.VMEM((LANES, hid), bf),
-        pltpu.VMEM((hid, rank), bf),
+        pltpu.VMEM((rank, hid), bf),
         pltpu.VMEM((LANES, width), bf),
         pltpu.VMEM((rows, hid), f32),
         pltpu.VMEM((rows, hid), f32),
@@ -648,7 +637,7 @@
         pltpu.VMEM((rows, LANES), bf),
         pltpu.VMEM((width, rows), bf),
         pltpu.VMEM((rows, hid), bf),
-        pltpu.VMEM((rows, 2 * hid + LANES), bf),
+        pltpu.VMEM((rows, 2 * hid), bf),
         pltpu.VMEM((rows, LANES), f32),
         pltpu.VMEM((width, 2 * LANES), f32),
         pltpu.VMEM((share * n, LANES), f32),
@@ -661,7 +650,7 @@
         pltpu.VMEM((half, extra, LANES), bf),
         pltpu.VMEM((quarter, extra, LANES), bf),
         pltpu.VMEM((line - 1, extra, LANES), bf),
-        pltpu.SemaphoreType.DMA((12 + 3 * rep,)),
+        pltpu.SemaphoreType.DMA((11 + 3 * rep,)),
         pltpu.SemaphoreType.DMA((n,)),
         pltpu.SemaphoreType.DMA((n,)),
         pltpu.SemaphoreType.DMA((n,)),
@@ -677,17 +666,17 @@
         functools.partial(dense_kernel, n, line),
         out_shape=(
             jax.ShapeDtypeStruct((t, width), bf),
-            jax.ShapeDtypeStruct((t, top), bf),
+            jax.ShapeDtypeStruct((top, t), f32),
             jax.ShapeDtypeStruct((share, LANES), f32),
         ),
-        in_specs=[pl.BlockSpec(memory_space=pl.ANY)] * len(operands),
+        in_specs=[pl.BlockSpec(memory_space=pltpu.VMEM if i == 3 else pl.ANY) for i in range(13)],
         out_specs=(pl.BlockSpec(memory_space=pltpu.VMEM),) * 3,
         scratch_shapes=scratch,
         compiler_params=pltpu.CompilerParams(
-            collective_id=0, has_side_effects=True, vmem_limit_bytes=50 * 1024 * 1024
+            collective_id=0, has_side_effects=True, vmem_limit_bytes=62 * 1024 * 1024
         ),
-    )(*operands)
-    return grad_in, grad_combine, adapters.reshape(-1)
+    )(grad, tok, routes.T, combine.T, gate, upper, down, gal.T, gar, ual.T, uar, dal.T, dar)
+    return grad_in, grad_combine.astype(bf).T, adapters.reshape(-1)
 
 
 def dense_fits(tokens, routes, gate, rank, groups, n):

time: 64.2 us -> 57.8 us (0.900)
  local copies, waits for them, and re-layouts: 10.5 us -> 2.86 us
  other arithmetic: 0 us -> 1.25 us
    unnamed x18 -> x2, local copies, waits for them, and re-layouts: 10.5 us -> 2.86 us
    transpose x0 -> x1, other arithmetic: none -> 1.25 us  [dense_shards(): return (grad_in, grad_combine.astype(bf).T, adapters.reshape(-1))]
where the time goes in v2:
time: 57.8 us; the launch traced here: 57.5 us
  Pallas kernels  52.8 us (91%)
  local copies, waits for them, and re-layouts  2.86 us (5%)
  other arithmetic  1.25 us (2%)
  between operations  0.64 us (1%)
    pallas_call x1, Pallas kernels, dense_shards(): pl.pallas_call(functools.partial(dense_kernel, n, line), out_shape=(jax.S...  52.8 us
    unnamed x2, local copies, waits for them, and re-layouts  2.86 us
    transpose x1, other arithmetic, dense_shards(): return (grad_in, grad_combine.astype(bf).T, adapters.reshape(-1))  1.25 us

profile of v2, /device:TPU:0, one launch (start us, length us, event | category | flops | bytes accessed | tf_op | source)
XLA Modules:
  0.0 57.5 jit_solution(18075263709116571588)
XLA Ops:
  0.6 52.8 %shard_map.148 = (bf16[16,2048]{1,0:T(8,128)(2,1)}, f32[8,16]{1,0:T(8,128)}, f32[66,128]{1,0:T(8,128)}) custom-call(bf16[16,2048]{1,0:T(8,128)(2,1)} %grad_hbm.1, bf16[16,2048]{1,0:T(8,128)(2,1)} %tok_hbm.1, s32[8,16]{1,0:T(8,128)} %bitcast.12, bf16[8,16]{1,0:T(8,128)(2,1)} %bitcast.13, bf16[1,2048,768]{2,1,0:T(8,128)(2,1)} %gate_hbm.1, ...), custom_call_target="tpu_custom_call" | custom-call | tf_op jit(solution)/shard_map/pallas_call | solution.py:665
  53.4 1.3 %convert_bitcast_fusion = bf16[16,8]{0,1:T(8,128)(2,1)} fusion(f32[8,16]{1,0:T(8,128)} %get-tuple-element.7), kind=kLoop, calls=%fused_computation | loop fusion | flops 128 | bytes 768 | tf_op jit(solution)/shard_map/transpose | solution.py:679
  54.7 1.5 %copy.18 = bf16[16,2048]{1,0:T(8,128)(2,1)} copy(bf16[16,2048]{1,0:T(8,128)(2,1)} %get-tuple-element.12) | data formatting | bytes 131072
  56.1 1.4 %copy.19 = f32[8448]{0:T(1024)} copy(f32[8448]{0:T(1024)} %bitcast.10) | data formatting | bytes 67584

commit v3 on v2

--- a/solution.py
+++ b/solution.py
@@ -237,7 +237,8 @@
 
 
 MESH = pl.DeviceIdType.MESH
-CHUNKS = 4
+CHUNKS = 2
+PARTS = 2
 LANES = 128
 
 
@@ -365,12 +366,12 @@
         pl.semaphore_signal(barrier, inc=1, device_id={"exp": peer}, device_id_type=MESH)
     pl.semaphore_wait(barrier, len(peers))
 
-    def gather_copy(buf, send, recv, src, dst, peer):
+    def gather_copy(buf, first, size, part, send, recv, src, dst, peer):
         return pltpu.make_async_remote_copy(
-            src_ref=buf.at[src],
-            dst_ref=buf.at[dst],
-            send_sem=send.at[dst],
-            recv_sem=recv.at[dst],
+            src_ref=buf.at[src, :, pl.ds(first, size)],
+            dst_ref=buf.at[dst, :, pl.ds(first, size)],
+            send_sem=send.at[part, dst],
+            recv_sem=recv.at[part, dst],
             device_id={"exp": peer},
             device_id_type=MESH,
         )
@@ -408,9 +409,14 @@
         for s in range(half, n):
             arrived(bufs, s)
 
-    xb, gb = (xbuf, xs, xr), (gbuf, gs, gr)
+    size = width // PARTS
+    x_parts = [(xbuf, i * size, size, i, xs, xr) for i in range(PARTS)]
+    g_parts = [
+        (gbuf, i * size, size + (LANES if i == PARTS - 1 else 0), i, gs, gr) for i in range(PARTS)
+    ]
     own_x.wait()
-    own_phase(xb)
+    for part in x_parts:
+        own_phase(part)
     own_g.wait()
     own_r.wait()
     lanes_t = lax.broadcasted_iota(jnp.int32, (t, LANES), 1)
@@ -420,32 +426,40 @@
     for k in range(top):
         dense = dense + jnp.where(lanes_t == chosen[:, k : k + 1], weights[:, k : k + 1], 0.0)
     gbuf[0, :, pl.ds(width, LANES)] = dense.astype(jnp.bfloat16)
-    own_phase(gb)
 
     rcat[pl.ds(0, rank), pl.ds(hid, hid)] = jnp.zeros((rank, hid), jnp.bfloat16)
     rcat[pl.ds(rank, rank), pl.ds(0, hid)] = jnp.zeros((rank, hid), jnp.bfloat16)
     ashare[...] = jnp.zeros_like(ashare)
-    line_phase(xb)
-    across_phase(xb)
+    for i in range(PARTS):
+        line_phase(x_parts[i])
+        own_phase(g_parts[i])
+        if i > 0:
+            across_phase(x_parts[i - 1])
+    line_phase(g_parts[0])
+    across_phase(x_parts[PARTS - 1])
     for copy in load_al + load_rc:
         copy.wait()
     load_gate.wait()
     load_upper.wait()
-    sibling_phase(xb)
-
-    line_phase(gb)
+    for part in x_parts:
+        sibling_phase(part)
+
     x_all = xbuf[...].reshape(rows, width)
     low_cat = nt(x_all, left[...]).astype(jnp.bfloat16)
     pre_g[...] = nn(x_all, wcat[:, pl.ds(0, hid)]) + adapter_scale * nn(low_cat, rcat[:, pl.ds(0, hid)])
-    across_phase(gb)
+    for i in range(1, PARTS):
+        line_phase(g_parts[i])
+        across_phase(g_parts[i - 1])
     pre_u[...] = nn(x_all, wcat[:, pl.ds(hid, hid)]) + adapter_scale * nn(
         low_cat, rcat[:, pl.ds(hid, hid)]
     )
+    across_phase(g_parts[PARTS - 1])
     xt[...] = x_all.T
     for copy in load_small:
         copy.wait()
     load_down.wait()
-    sibling_phase(gb)
+    for part in g_parts:
+        sibling_phase(part)
 
     g_all = gbuf[:, :, pl.ds(0, width)].reshape(rows, width)
     gates = gbuf[:, :, pl.ds(width, LANES)].reshape(rows, LANES).astype(jnp.float32)
@@ -577,7 +591,7 @@
                         jnp.bfloat16
                     )
 
-    plan = list(range(CHUNKS)) + [CHUNKS]
+    plan = [0, CHUNKS] + list(range(1, CHUNKS))
     for k in range(len(plan) + 2):
         if k < len(plan):
             if plan[k] < CHUNKS:
@@ -651,10 +665,10 @@
         pltpu.VMEM((quarter, extra, LANES), bf),
         pltpu.VMEM((line - 1, extra, LANES), bf),
         pltpu.SemaphoreType.DMA((11 + 3 * rep,)),
-        pltpu.SemaphoreType.DMA((n,)),
-        pltpu.SemaphoreType.DMA((n,)),
-        pltpu.SemaphoreType.DMA((n,)),
-        pltpu.SemaphoreType.DMA((n,)),
+        pltpu.SemaphoreType.DMA((PARTS, n)),
+        pltpu.SemaphoreType.DMA((PARTS, n)),
+        pltpu.SemaphoreType.DMA((PARTS, n)),
+        pltpu.SemaphoreType.DMA((PARTS, n)),
         pltpu.SemaphoreType.DMA((CHUNKS + 1,)),
         pltpu.SemaphoreType.DMA((CHUNKS + 1,)),
         pltpu.SemaphoreType.DMA((CHUNKS + 1,)),

time: 57.8 us -> 54.2 us (0.938)
  Pallas kernels: 52.8 us -> 49.2 us
    pallas_call x1, Pallas kernels: 52.8 us -> 49.2 us  [dense_shards(): pl.pallas_call(functools.partial(dense_kernel, n, line), out_shape=(jax.S...]
where the time goes in v3:
time: 54.2 us; the launch traced here: 53.9 us
  Pallas kernels  49.2 us (91%)
  local copies, waits for them, and re-layouts  2.86 us (5%)
  other arithmetic  1.25 us (2%)
  between operations  0.64 us (1%)
    pallas_call x1, Pallas kernels, dense_shards(): pl.pallas_call(functools.partial(dense_kernel, n, line), out_shape=(jax.S...  49.2 us
    unnamed x2, local copies, waits for them, and re-layouts  2.86 us
    transpose x1, other arithmetic, dense_shards(): return (grad_in, grad_combine.astype(bf).T, adapters.reshape(-1))  1.25 us

profile of v3, /device:TPU:0, one launch (start us, length us, event | category | flops | bytes accessed | tf_op | source)
XLA Modules:
  0.0 53.9 jit_solution(11746853661710912573)
XLA Ops:
  0.6 49.2 %shard_map.148 = (bf16[16,2048]{1,0:T(8,128)(2,1)}, f32[8,16]{1,0:T(8,128)}, f32[66,128]{1,0:T(8,128)}) custom-call(bf16[16,2048]{1,0:T(8,128)(2,1)} %grad_hbm.1, bf16[16,2048]{1,0:T(8,128)(2,1)} %tok_hbm.1, s32[8,16]{1,0:T(8,128)} %bitcast.12, bf16[8,16]{1,0:T(8,128)(2,1)} %bitcast.13, bf16[1,2048,768]{2,1,0:T(8,128)(2,1)} %gate_hbm.1, ...), custom_call_target="tpu_custom_call" | custom-call | tf_op jit(solution)/shard_map/pallas_call | solution.py:679
  49.8 1.3 %convert_bitcast_fusion = bf16[16,8]{0,1:T(8,128)(2,1)} fusion(f32[8,16]{1,0:T(8,128)} %get-tuple-element.7), kind=kLoop, calls=%fused_computation | loop fusion | flops 128 | bytes 768 | tf_op jit(solution)/shard_map/transpose | solution.py:693
  51.1 1.5 %copy.18 = bf16[16,2048]{1,0:T(8,128)(2,1)} copy(bf16[16,2048]{1,0:T(8,128)(2,1)} %get-tuple-element.12) | data formatting | bytes 131072
  52.6 1.4 %copy.19 = f32[8448]{0:T(1024)} copy(f32[8448]{0:T(1024)} %bitcast.10) | data formatting | bytes 67584
